TPU v7x, 512 devices: a whole 4x8x8 slice. The times are simulated.
512 devices in a mesh: patch: 4 (over x), curve: 128 (over z, y, core).
Axes of the slice: x: 4, y: 8, z: 8, core: 2. Of those that a mesh axis runs over, the one named last changes fastest.
Arguments:
- points: bfloat16 [128, 4, 256, 512], P('curve', 'patch'), may hold values from -6 to 6
- norm_gain_one: float32 [512], replicated, may hold values from 0.4 to 2.5, as said below
- qkv_one: bfloat16 [512, 1536], replicated, may hold values from -0.25 to 0.25
- out_one: bfloat16 [512, 512], replicated, may hold values from -0.25 to 0.25
- hilbert_pos: int32 [128, 4, 256], P('curve', 'patch'), may hold values from 0 to 32767, as said below
- norm_gain_two: float32 [512], replicated, may hold values from 0.4 to 2.5, as said below
- qkv_two: bfloat16 [512, 1536], replicated, may hold values from -0.25 to 0.25
- out_two: bfloat16 [512, 512], replicated, may hold values from -0.25 to 0.25
- hilbert_seg: int32 [4, 128, 256], P('patch', 'curve'), may hold values from 0 to 7, never falling along the last dimension, each value on 1 to 128 neighbouring positions
- out_grad: bfloat16 [4, 128, 256, 512], P('patch', 'curve'), may hold values from -6 to 6
Outputs:
- point_grad: bfloat16 [128, 4, 256, 512], P('curve', 'patch')
Inputs may be any that keep to these rules, and one draw needn't show every extreme that they name: `hilbert_pos`: for each index p of the second dimension, the values over all c and i form a permutation of 0 to 32767. From the points of one device at most 4 have q // 256 equal to any one value, and in every draw some device sends exactly 4 to some owner. `hilbert_seg`: within one device's slots the numbers never fall; a patch holds at most 128 slots. `norm_gain_one`: positive gains. `norm_gain_two`: positive gains.
All inputs are finite; a program needn't handle non-finite values.
Results may differ from a plain program's by a relative error of at most 0.02.
Values may be sent and summed in bfloat16 or wider, within the bound.
A program may use at most 64 MiB of HBM per device.

v0:
```python
import jax
import jax.numpy as jnp
from jax import lax
from jax.sharding import PartitionSpec as P

HEADS = 16
EPS = 1e-06


def prepare(source_rows, gain, w_qkv):
    wide = source_rows.astype(jnp.float32)
    power = jnp.mean(wide * wide, axis=-1, keepdims=True)
    normed = (wide * lax.rsqrt(power + EPS) * gain).astype(jnp.bfloat16)
    return jnp.dot(normed, w_qkv, preferred_element_type=jnp.float32).astype(jnp.bfloat16)


def finish(source_rows, mixed, w_out):
    total = source_rows.astype(jnp.float32) + jnp.dot(
        mixed, w_out, preferred_element_type=jnp.float32
    )
    return total.astype(jnp.bfloat16)


def attend(queries, keys, values, allowed):
    count, width = queries.shape
    depth = width // HEADS
    q_heads = queries.astype(jnp.float32).reshape(count, HEADS, depth)
    k_heads = keys.astype(jnp.float32).reshape(-1, HEADS, depth)
    v_heads = values.astype(jnp.float32).reshape(-1, HEADS, depth)
    scores = jnp.einsum("rhe,khe->hrk", q_heads, k_heads) * depth ** (-0.5)
    scores = jnp.where(allowed[None], scores, -1e30)
    weights = jax.nn.softmax(scores, axis=-1)
    rounded = lax.optimization_barrier(weights.astype(jnp.bfloat16))
    mixed = jnp.einsum("hrk,khe->rhe", rounded.astype(jnp.float32), v_heads)
    return mixed.reshape(count, width).astype(jnp.bfloat16)


def device_block(source_rows, segment, gain, w_qkv, w_out):
    width = source_rows.shape[1]
    packed = prepare(source_rows, gain, w_qkv)
    allowed = segment[:, None] == segment[None, :]
    mixed = attend(packed[:, :width], packed[:, width : 2 * width], packed[:, 2 * width :], allowed)
    return finish(source_rows, mixed, w_out)


def head_view(matrix, index, block, depth):
    columns = block * depth
    piece = lax.dynamic_slice_in_dim(matrix, index * columns, columns, 1)
    return piece.reshape(matrix.shape[0], block, depth)


def regroup(stacked):
    groups, length, columns = stacked.shape
    return jnp.transpose(stacked, (1, 0, 2)).reshape(length, groups * columns)


def round_trip(values):
    return lax.optimization_barrier(values.astype(jnp.bfloat16)).astype(jnp.float32)


def shards(
    points,
    norm_gain_one,
    qkv_one,
    out_one,
    hilbert_pos,
    norm_gain_two,
    qkv_two,
    out_two,
    hilbert_seg,
    out_grad,
):
    count = points.shape[2]
    width = points.shape[3]
    depth = width // HEADS
    block = 4
    groups = HEADS // block
    scale = depth ** (-0.5)
    source_rows = points.reshape(count, width)
    packed, prep_pull = jax.vjp(lambda inputs: prepare(inputs, norm_gain_one, qkv_one), source_rows)
    queries = packed[:, :width]
    gathered = lax.all_gather(packed[:, width:], "patch", axis=0, tiled=True)
    keys_all = gathered[:, :width]
    values_all = gathered[:, width:]
    patch_len = gathered.shape[0]

    def forward_group(index):
        q_part = head_view(queries, index, block, depth)
        k_part = head_view(keys_all, index, block, depth)
        v_part = head_view(values_all, index, block, depth)
        scores = (
            jnp.einsum("rhe,khe->hrk", q_part, k_part, preferred_element_type=jnp.float32) * scale
        )
        weights = jax.nn.softmax(scores, axis=-1).astype(jnp.bfloat16)
        mixed_part = jnp.einsum("hrk,khe->rhe", weights, v_part, preferred_element_type=jnp.float32)
        return mixed_part.reshape(count, block * depth)

    mixed = regroup(lax.map(forward_group, jnp.arange(groups))).astype(jnp.bfloat16)
    moved, finish_pull = jax.vjp(
        lambda inputs, mix: finish(inputs, mix, out_one), source_rows, mixed
    )
    curve_size = lax.axis_size("curve")
    capacity = 2 * count // curve_size
    target = hilbert_pos.reshape(count)
    owner = target // count
    offset = target % count
    columns = jnp.arange(curve_size, dtype=jnp.int32)
    onehot = (owner[:, None] == columns[None, :]).astype(jnp.bfloat16)
    earlier = (
        lax.broadcasted_iota(jnp.int32, (count, count), 0)
        > lax.broadcasted_iota(jnp.int32, (count, count), 1)
    ).astype(jnp.bfloat16)
    before = jnp.dot(earlier, onehot, preferred_element_type=jnp.float32)
    ranking = jnp.sum(before * onehot.astype(jnp.float32), axis=1).astype(jnp.int32)
    slot = owner * capacity + ranking
    outgoing = jnp.zeros((curve_size * capacity, width), jnp.bfloat16).at[slot].set(moved)
    outgoing_at = jnp.full((curve_size * capacity,), count, jnp.int32).at[slot].set(offset)
    arrived, arrived_at = (
        lax.all_to_all(
            outgoing.reshape(curve_size, capacity, width),
            "curve",
            split_axis=0,
            concat_axis=0,
            tiled=True,
        ),
        lax.all_to_all(
            outgoing_at.reshape(curve_size, capacity),
            "curve",
            split_axis=0,
            concat_axis=0,
            tiled=True,
        ),
    )
    landing = arrived_at.reshape(-1)
    hilbert_rows = (
        jnp.zeros((count, width), jnp.bfloat16)
        .at[landing]
        .set(arrived.reshape(-1, width), mode="drop")
    )
    segment = hilbert_seg.reshape(count)
    _, second_pull = jax.vjp(
        lambda inputs: device_block(inputs, segment, norm_gain_two, qkv_two, out_two), hilbert_rows
    )
    (hilbert_grad,) = second_pull(out_grad.reshape(count, width))
    valid = landing < count
    clipped = jnp.minimum(landing, count - 1)
    returning = jnp.where(
        valid[:, None], jnp.take(hilbert_grad, clipped, axis=0), jnp.zeros((), jnp.bfloat16)
    )
    arrived_home = lax.all_to_all(
        returning.reshape(curve_size, capacity, width),
        "curve",
        split_axis=0,
        concat_axis=0,
        tiled=True,
    )
    moved_grad = arrived_home.reshape(-1, width)[slot]
    residual_grad, mixed_grad = finish_pull(moved_grad)

    def backward_group(index):
        q_part = head_view(queries, index, block, depth)
        k_part = head_view(keys_all, index, block, depth)
        v_part = head_view(values_all, index, block, depth)
        g_part = head_view(mixed_grad, index, block, depth)
        scores = (
            jnp.einsum("rhe,khe->hrk", q_part, k_part, preferred_element_type=jnp.float32) * scale
        )
        weights = jax.nn.softmax(scores, axis=-1)
        rounded = weights.astype(jnp.bfloat16)
        weight_grad = round_trip(
            jnp.einsum("rhe,khe->hrk", g_part, v_part, preferred_element_type=jnp.float32)
        )
        score_grad = (
            weights * (weight_grad - jnp.sum(weights * weight_grad, axis=-1, keepdims=True)) * scale
        )
        query_grad = jnp.einsum("hrk,khe->rhe", score_grad, k_part.astype(jnp.float32)).reshape(
            count, block * depth
        )
        key_grad = jnp.einsum("hrk,rhe->khe", score_grad, q_part.astype(jnp.float32)).reshape(
            patch_len, block * depth
        )
        value_grad = jnp.einsum(
            "hrk,rhe->khe", rounded, g_part, preferred_element_type=jnp.float32
        ).reshape(patch_len, block * depth)
        return (query_grad, key_grad, value_grad)

    query_parts, key_parts, value_parts = lax.map(backward_group, jnp.arange(groups))
    query_grad = regroup(query_parts).astype(jnp.bfloat16)
    key_sum, value_sum = (
        lax.psum_scatter(regroup(key_parts), "patch", scatter_dimension=0, tiled=True),
        lax.psum_scatter(regroup(value_parts), "patch", scatter_dimension=0, tiled=True),
    )
    key_grad = key_sum.astype(jnp.bfloat16)
    value_grad = value_sum.astype(jnp.bfloat16)
    packed_grad = jnp.concatenate([query_grad, key_grad, value_grad], axis=1)
    (path_grad,) = prep_pull(packed_grad)
    total_grad = residual_grad + path_grad
    return total_grad.reshape(points.shape)


def solution(mesh):
    in_specs = (
        P("curve", "patch", None, None),
        P(),
        P(),
        P(),
        P("curve", "patch", None),
        P(),
        P(),
        P(),
        P("patch", "curve", None),
        P("patch", "curve", None, None),
    )
    out_specs = P("curve", "patch", None, None)
    return jax.shard_map(shards, mesh=mesh, in_specs=in_specs, out_specs=out_specs, check_vma=False)
```

profile of v0, /device:TPU:1, one launch (start us, length us, event | category | flops | bytes accessed | tf_op | source)
XLA Modules:
  0.0 356.9 jit_solution(2144473138300720519)
XLA Ops:
  9.0 2.1 convolution_convert_fusion.2
  14.4 18.4 %all-to-all-start = ((s32[128,1,4]{2,1,0:T(1,128)}), s32[128,1,4]{2,1,0:T(1,128)S(1)}, u32[]{:S(2)}, u32[]{:S(2)}) async-start(s32[128,1,4]{2,1,0:T(1,128)} %bitcast.21), calls=%async_computation | async-start | bytes 131072 | tf_op jit(solution)/shard_map/all_to_all | solution.py:126
  34.7 19.1 %all-gather.2.cloned.1.call-done = bf16[1024,1024]{1,0:T(8,128)(2,1)} async-done(((bf16[256,1024]{1,0:T(8,128)(2,1)}), bf16[1024,1024]{1,0:T(8,128)(2,1)}) %all-gather.2.cloned.1.call-update) | async-done | bytes 2097168 | tf_op jit(solution)/shard_map/all_gather | solution.py:82
  53.8 3.0 fusion.100
  56.8 1.5 copy.81
  58.3 2.3 copy.83
  61.3 40.3 %while.24 = (s32[]{:T(128)}, bf16[4,256,128]{1,2,0:T(8,128)(2,1)}, s32[4]{0:T(128)S(1)}, bf16[1024,512]{0,1:T(8,128)(2,1)S(1)}, bf16[256,512]{0,1:T(8,128)(2,1)}...) while((s32[]{:T(128)}, bf16[4,256,128]{1,2,0:T(8,128)(2,1)}, ...), condition=%wide.region_6.7_spmd, body=%wide.region_3.6_spmd.sunk | while | flops 139461632 | bytes 10363059 | solution.py:98
  64.4 3.4 fusion.159
  67.7 3.0 fusion.160
  74.5 3.4 fusion.159
  77.8 3.0 fusion.160
  84.5 3.4 fusion.159
  87.9 3.0 fusion.160
  94.6 3.4 fusion.159
  98.0 3.0 fusion.160
  101.6 2.1 fusion.43
  103.8 2.1 scatter_custom_fusion.1
  106.8 14.7 %all-to-all-start.1 = ((bf16[128,4,512]{2,1,0:T(4,128)(2,1)}), bf16[128,4,512]{2,1,0:T(4,128)(2,1)}, u32[]{:S(2)}, u32[]{:S(2)}) async-start(bf16[128,4,512]{2,1,0:T(4,128)(2,1)} %reshape.360), calls=%async_computation.1 | async-start | bytes 1048576 | tf_op jit(solution)/shard_map/all_to_all | solution.py:119
  125.1 16.6 %all-to-all-done.1 = bf16[128,4,512]{2,1,0:T(4,128)(2,1)} async-done(((bf16[128,4,512]{2,1,0:T(4,128)(2,1)}), bf16[128,4,512]{2,1,0:T(4,128)(2,1)}, u32[]{:S(2)}, u32[]{:S(2)}) %all-to-all-start.1) | async-done | bytes 524320 | tf_op jit(solution)/shard_map/all_to_all | solution.py:119
  141.8 2.0 reshape.406
  143.8 2.9 scatter_custom_fusion.2
  148.4 1.8 copy.85
  150.1 1.8 copy.84
  151.9 1.8 copy.87
  153.7 3.0 convolution_convert_fusion.3
  156.8 4.5 %fusion.102 = (f32[16,256]{1,0:T(8,128)S(1)}, f32[16,256,256]{1,2,0:T(8,128)}) fusion(pred[256,256]{0,1:T(8,128)(4,1)} %broadcast_compare_fusion, bf16[256,16,32]{0,2,1:T(8,128)(2,1)} %bitcast.185, bf16[256,16,32]{0,2,1:T(8,128)(2,1)} %bitcast.187), kind=kOutput, calls=%fused_computation.171 | convolution fusion | flops 71303424 | bytes 4800512 | tf_op jit(solution)/shard_map/jvp()/sub | solution.py:32
  161.3 4.0 %divide_convert_fusion.2 = (bf16[16,256,256]{1,2,0:T(8,128)(2,1)S(1)}, f32[16,256]{1,0:T(8,128)S(1)}) fusion(f32[16,256,256]{1,2,0:T(8,128)} %get-tuple-element.217, f32[16,256]{1,0:T(8,128)S(1)} %get-tuple-element.216, f32[16,256]{1,0:T(8,128)S(1)} %multiply_divide_fusion, bf16[16,256,256]{1,2,0:T(8,128)(2,1)} %convolution_convert_fusion.3), kind=kLoop, calls=%fused_computation.58 | loop fusion | flops 6287360 | bytes 8437760 | tf_op jit(solution)/shard_map/jvp()/convert_element_type | solution.py:33
  169.9 2.6 gather_fusion
  175.1 6.6 %all-to-all-start.2 = ((bf16[128,4,512]{2,1,0:T(4,128)(2,1)}), bf16[128,4,512]{2,1,0:T(4,128)(2,1)}, u32[]{:S(2)}, u32[]{:S(2)}) async-start(bf16[128,4,512]{2,1,0:T(4,128)(2,1)} %select_select_fusion), calls=%async_computation.2 | async-start | bytes 1048576 | tf_op jit(solution)/shard_map/all_to_all | solution.py:150
  181.8 19.7 %all-to-all-done.2 = bf16[128,4,512]{2,1,0:T(4,128)(2,1)} async-done(((bf16[128,4,512]{2,1,0:T(4,128)(2,1)}), bf16[128,4,512]{2,1,0:T(4,128)(2,1)}, u32[]{:S(2)}, u32[]{:S(2)}) %all-to-all-start.2) | async-done | bytes 524320 | tf_op jit(solution)/shard_map/all_to_all | solution.py:150
  202.6 1.9 gather_fusion.1
  204.5 2.1 convolution_convert_fusion.5
  207.3 74.5 %while.25 = (s32[]{:T(128)}, bf16[4,256,128]{1,2,0:T(8,128)(2,1)}, f32[4,1024,128]{1,2,0:T(8,128)}, f32[4,1024,128]{1,2,0:T(8,128)}, s32[4]{0:T(128)S(1)}, /*ind...) while((s32[]{:T(128)}, bf16[4,256,128]{1,2,0:T(8,128)(2,1)}, ...), condition=%wide.region_18.19_spmd, body=%wide.region_14.18_spmd.sunk | while | flops 356515840 | bytes 60391696 | solution.py:187
  210.5 2.1 convolution_convert_fusion.12
  213.4 3.4 fusion.171
  216.8 3.7 %fusion.172 = f32[4,256]{1,0:T(4,128)S(1)} fusion(bf16[4,256,1024]{2,1,0:T(8,128)(2,1)} %convolution_convert_fusion.12, f32[4,256,1024]{2,1,0:T(8,128)} %get-tuple-element.326, f32[4,256]{1,0:T(4,128)S(1)} %get-tuple-element.327), kind=kLoop, calls=%fused_computation.21.clone.1 | loop fusion | flops 4193280 | bytes 6299648 | tf_op jit(solution)/shard_map/while/body/eval_jaxpr/reduce_sum | solution.py:174
  229.1 2.1 convolution_convert_fusion.12
  232.1 3.3 fusion.171
  235.4 3.7 %fusion.172 = f32[4,256]{1,0:T(4,128)S(1)} fusion(bf16[4,256,1024]{2,1,0:T(8,128)(2,1)} %convolution_convert_fusion.12, f32[4,256,1024]{2,1,0:T(8,128)} %get-tuple-element.326, f32[4,256]{1,0:T(4,128)S(1)} %get-tuple-element.327), kind=kLoop, calls=%fused_computation.21.clone.1 | loop fusion | flops 4193280 | bytes 6299648 | tf_op jit(solution)/shard_map/while/body/eval_jaxpr/reduce_sum | solution.py:174
  247.7 2.1 convolution_convert_fusion.12
  250.7 3.4 fusion.171
  254.0 3.7 %fusion.172 = f32[4,256]{1,0:T(4,128)S(1)} fusion(bf16[4,256,1024]{2,1,0:T(8,128)(2,1)} %convolution_convert_fusion.12, f32[4,256,1024]{2,1,0:T(8,128)} %get-tuple-element.326, f32[4,256]{1,0:T(4,128)S(1)} %get-tuple-element.327), kind=kLoop, calls=%fused_computation.21.clone.1 | loop fusion | flops 4193280 | bytes 6299648 | tf_op jit(solution)/shard_map/while/body/eval_jaxpr/reduce_sum | solution.py:174
  266.3 2.1 convolution_convert_fusion.12
  269.3 3.4 fusion.171
  272.6 3.7 %fusion.172 = f32[4,256]{1,0:T(4,128)S(1)} fusion(bf16[4,256,1024]{2,1,0:T(8,128)(2,1)} %convolution_convert_fusion.12, f32[4,256,1024]{2,1,0:T(8,128)} %get-tuple-element.326, f32[4,256]{1,0:T(4,128)S(1)} %get-tuple-element.327), kind=kLoop, calls=%fused_computation.21.clone.1 | loop fusion | flops 4193280 | bytes 6299648 | tf_op jit(solution)/shard_map/while/body/eval_jaxpr/reduce_sum | solution.py:174
  282.6 25.7 %reduce-scatter.5.cloned.1.call-done = f32[256,512]{0,1:T(8,128)} async-done(((f32[1024,512]{0,1:T(8,128)}), f32[256,512]{0,1:T(8,128)}) %reduce-scatter.5.cloned.1.call-update) | async-done | bytes 524304 | tf_op jit(solution)/shard_map/reduce_scatter | solution.py:191
  309.4 36.8 %reduce-scatter.3.cloned.1.call-done = f32[256,512]{0,1:T(8,128)} async-done(((f32[1024,512]{0,1:T(8,128)}), f32[256,512]{0,1:T(8,128)}) %reduce-scatter.3.cloned.1.call-update) | async-done | bytes 524304 | tf_op jit(solution)/shard_map/reduce_scatter | solution.py:190
  347.3 2.1 fusion.68
  (173 shorter events, 75.0 us)
Async XLA Ops:
  6.5 140.3 %copy-start = (bf16[512,1536]{1,0:T(8,128)(2,1)S(1)}, bf16[512,1536]{1,0:T(8,128)(2,1)}, u32[]{:S(2)}) copy-start(bf16[512,1536]{1,0:T(8,128)(2,1)} %param.20) | copy-start | bytes 4718596
  6.5 5.5 %copy-start.18 = (s32[1,1,256]{2,1,0:T(1,128)S(1)}, s32[1,1,256]{2,1,0:T(1,128)}, u32[]{:S(2)}) copy-start(s32[1,1,256]{2,1,0:T(1,128)} %param.18) | copy-start | bytes 3076
  6.5 27.2 %copy-start.9 = (bf16[512,512]{1,0:T(8,128)(2,1)S(1)}, bf16[512,512]{1,0:T(8,128)(2,1)}, u32[]{:S(2)}) copy-start(bf16[512,512]{1,0:T(8,128)(2,1)} %param.21) | copy-start | bytes 1572868
  6.5 27.2 %copy-start.7 = (bf16[1,1,256,512]{3,2,1,0:T(8,128)(2,1)S(1)}, bf16[1,1,256,512]{3,2,1,0:T(8,128)(2,1)}, u32[]{:S(2)}) copy-start(bf16[1,1,256,512]{3,2,1,0:T(8,128)(2,1)} %param.23) | copy-start | bytes 786436
  6.5 47.3 %all-gather.2.cloned.1.call-start = ((), (), s32[]{:S(2)}) async-start(), calls=%async_computation.5 | async-start | bytes 2621440 | tf_op jit(solution)/shard_map/all_gather | solution.py:82
  7.8 0.6 copy-start.16
  8.4 0.6 copy-start.14
  14.4 92.4 %all-to-all-start = ((s32[128,1,4]{2,1,0:T(1,128)}), s32[128,1,4]{2,1,0:T(1,128)S(1)}, u32[]{:S(2)}, u32[]{:S(2)}) async-start(s32[128,1,4]{2,1,0:T(1,128)} %bitcast.21), calls=%async_computation | async-start | bytes 131072 | tf_op jit(solution)/shard_map/all_to_all | solution.py:126
  61.3 40.4 %copy-start.5 = (bf16[1,1,256,512]{3,2,1,0:T(8,128)(2,1)S(1)}, bf16[1,1,256,512]{3,2,1,0:T(8,128)(2,1)}, u32[]{:S(2)}) copy-start(bf16[1,1,256,512]{3,2,1,0:T(8,128)(2,1)} %param.14) | copy-start | bytes 786436
  61.3 60.3 %copy-start.19 = (s32[1,1,256]{2,1,0:T(1,128)S(1)}, s32[1,1,256]{2,1,0:T(1,128)}, u32[]{:S(2)}) copy-start(s32[1,1,256]{2,1,0:T(1,128)} %param.22) | copy-start | bytes 3076
  101.6 45.2 %copy-start.20 = (f32[512]{0:T(512)S(1)}, f32[512]{0:T(512)}, u32[]{:S(2)}) copy-start(f32[512]{0:T(512)} %param.19) | copy-start | bytes 6148
  106.8 35.0 %all-to-all-start.1 = ((bf16[128,4,512]{2,1,0:T(4,128)(2,1)}), bf16[128,4,512]{2,1,0:T(4,128)(2,1)}, u32[]{:S(2)}, u32[]{:S(2)}) async-start(bf16[128,4,512]{2,1,0:T(4,128)(2,1)} %reshape.360), calls=%async_computation.1 | async-start | bytes 1048576 | tf_op jit(solution)/shard_map/all_to_all | solution.py:119
  161.2 4.0 %copy-start.3 = (bf16[16,256,256]{1,2,0:T(8,128)(2,1)S(1)}, bf16[16,256,256]{1,2,0:T(8,128)(2,1)}, u32[]{:S(2)}) copy-start(bf16[16,256,256]{1,2,0:T(8,128)(2,1)} %convolution_convert_fusion.3) | copy-start | bytes 6291460
  161.2 4.7 %copy-start.4 = (f32[16,256,256]{1,2,0:T(8,128)S(1)}, f32[16,256,256]{1,2,0:T(8,128)}, u32[]{:S(2)}) copy-start(f32[16,256,256]{1,2,0:T(8,128)} %get-tuple-element.217) | copy-start | bytes 12582916
  161.3 4.7 %copy-start.11 = (bf16[256,512]{0,1:T(8,128)(2,1)S(1)}, bf16[256,512]{0,1:T(8,128)(2,1)}, u32[]{:S(2)}) copy-start(bf16[256,512]{0,1:T(8,128)(2,1)} %copy.85) | copy-start | bytes 786436
  161.3 4.7 %copy-start.13 = (pred[256,256]{0,1:T(8,128)(4,1)S(1)}, pred[256,256]{0,1:T(8,128)(4,1)}, u32[]{:S(2)}) copy-start(pred[256,256]{0,1:T(8,128)(4,1)} %broadcast_compare_fusion) | copy-start | bytes 196612
  165.9 1.2 copy-start.10
  168.3 1.5 copy-start.8
  175.1 26.4 %all-to-all-start.2 = ((bf16[128,4,512]{2,1,0:T(4,128)(2,1)}), bf16[128,4,512]{2,1,0:T(4,128)(2,1)}, u32[]{:S(2)}, u32[]{:S(2)}) async-start(bf16[128,4,512]{2,1,0:T(4,128)(2,1)} %select_select_fusion), calls=%async_computation.2 | async-start | bytes 1048576 | tf_op jit(solution)/shard_map/all_to_all | solution.py:150
  181.7 126.6 %reduce-scatter.5.cloned.1.call-start = ((), (), s32[]{:S(2)}) async-start(), calls=%async_computation.7 | async-start | bytes 2621440 | tf_op jit(solution)/shard_map/reduce_scatter | solution.py:191
  216.8 3.7 %copy-start.1 = (bf16[4,256,1024]{2,1,0:T(8,128)(2,1)S(1)}, bf16[4,256,1024]{2,1,0:T(8,128)(2,1)}, u32[]{:S(2)}) copy-start(bf16[4,256,1024]{2,1,0:T(8,128)(2,1)} %convolution_convert_fusion.12) | copy-start | bytes 6291460 | tf_op jit(solution)/shard_map/while
  216.8 4.7 %copy-start.2 = (f32[4,256,1024]{2,1,0:T(8,128)S(1)}, f32[4,256,1024]{2,1,0:T(8,128)}, u32[]{:S(2)}) copy-start(f32[4,256,1024]{2,1,0:T(8,128)} %get-tuple-element.326) | copy-start | bytes 12582916 | tf_op jit(solution)/shard_map/while
  235.4 3.7 %copy-start.1 = (bf16[4,256,1024]{2,1,0:T(8,128)(2,1)S(1)}, bf16[4,256,1024]{2,1,0:T(8,128)(2,1)}, u32[]{:S(2)}) copy-start(bf16[4,256,1024]{2,1,0:T(8,128)(2,1)} %convolution_convert_fusion.12) | copy-start | bytes 6291460 | tf_op jit(solution)/shard_map/while
  235.4 4.7 %copy-start.2 = (f32[4,256,1024]{2,1,0:T(8,128)S(1)}, f32[4,256,1024]{2,1,0:T(8,128)}, u32[]{:S(2)}) copy-start(f32[4,256,1024]{2,1,0:T(8,128)} %get-tuple-element.326) | copy-start | bytes 12582916 | tf_op jit(solution)/shard_map/while
  254.0 3.7 %copy-start.1 = (bf16[4,256,1024]{2,1,0:T(8,128)(2,1)S(1)}, bf16[4,256,1024]{2,1,0:T(8,128)(2,1)}, u32[]{:S(2)}) copy-start(bf16[4,256,1024]{2,1,0:T(8,128)(2,1)} %convolution_convert_fusion.12) | copy-start | bytes 6291460 | tf_op jit(solution)/shard_map/while
  254.0 4.7 %copy-start.2 = (f32[4,256,1024]{2,1,0:T(8,128)S(1)}, f32[4,256,1024]{2,1,0:T(8,128)}, u32[]{:S(2)}) copy-start(f32[4,256,1024]{2,1,0:T(8,128)} %get-tuple-element.326) | copy-start | bytes 12582916 | tf_op jit(solution)/shard_map/while
  272.6 3.7 %copy-start.1 = (bf16[4,256,1024]{2,1,0:T(8,128)(2,1)S(1)}, bf16[4,256,1024]{2,1,0:T(8,128)(2,1)}, u32[]{:S(2)}) copy-start(bf16[4,256,1024]{2,1,0:T(8,128)(2,1)} %convolution_convert_fusion.12) | copy-start | bytes 6291460 | tf_op jit(solution)/shard_map/while
  272.6 4.7 %copy-start.2 = (f32[4,256,1024]{2,1,0:T(8,128)S(1)}, f32[4,256,1024]{2,1,0:T(8,128)}, u32[]{:S(2)}) copy-start(f32[4,256,1024]{2,1,0:T(8,128)} %get-tuple-element.326) | copy-start | bytes 12582916 | tf_op jit(solution)/shard_map/while
  281.8 65.4 %copy-start.12 = (bf16[4,256,128]{1,2,0:T(8,128)(2,1)S(1)}, bf16[4,256,128]{1,2,0:T(8,128)(2,1)}, u32[]{:S(2)}) copy-start(bf16[4,256,128]{1,2,0:T(8,128)(2,1)} %get-tuple-element.87) | copy-start | bytes 786436
  281.8 65.4 %copy-start.21 = (f32[512]{0:T(512)S(1)}, f32[512]{0:T(512)}, u32[]{:S(2)}) copy-start(f32[512]{0:T(512)} %param.15) | copy-start | bytes 6148
  281.9 67.5 %copy-start.17 = (f32[256]{0:T(256)S(1)}, f32[256]{0:T(256)}, u32[]{:S(2)}) copy-start(f32[256]{0:T(256)} %copy-done.16) | copy-start | bytes 3076
  281.9 67.5 %copy-start.6 = (bf16[256,512]{1,0:T(8,128)(2,1)S(1)}, bf16[256,512]{1,0:T(8,128)(2,1)}, u32[]{:S(2)}) copy-start(bf16[256,512]{1,0:T(8,128)(2,1)} %gather_fusion.1) | copy-start | bytes 786436
  281.9 67.5 %copy-start.15 = (f32[256]{0:T(256)S(1)}, f32[256]{0:T(256)}, u32[]{:S(2)}) copy-start(f32[256]{0:T(256)} %copy-done.14) | copy-start | bytes 3076
  281.9 64.3 %reduce-scatter.3.cloned.1.call-start = ((), (), s32[]{:S(2)}) async-start(), calls=%async_computation.6 | async-start | bytes 2621440 | tf_op jit(solution)/shard_map/reduce_scatter | solution.py:190
Sparse Core Ops, SparseCore 0:
  12.1 41.6 all-gather.1
  282.0 26.2 reduce-scatter.4
  311.4 34.7 reduce-scatter.2
where the time goes:
time: 359 us; the launch traced here: 357 us
  waiting for transfers between devices  119 us (33%)
  matrix products  80.1 us (22%)
  local copies, waits for them, and re-layouts  73.3 us (20%)
  starting transfers between devices  39.9 us (11%)
  other arithmetic  26.5 us (7%)
  between operations  13.5 us (4%)
  loops' own time  5.05 us (1%)
    reduce_scatter x1, waiting for transfers between devices, shards(): lax.psum_scatter(regroup(key_parts), 'patch', scatter_dimension=0, tiled=...  36.8 us
    reduce_scatter x1, waiting for transfers between devices, shards(): lax.psum_scatter(regroup(value_parts), 'patch', scatter_dimension=0, tile...  25.7 us
    all_to_all x1, waiting for transfers between devices, shards(): lax.all_to_all(returning.reshape(curve_size, capacity, width), 'curve', s...  19.7 us
    all_gather x1, waiting for transfers between devices, shards(): gathered = lax.all_gather(packed[:, width:], 'patch', axis=0, tiled=True)  19.1 us
    dynamic_slice x28, local copies, waits for them, and re-layouts, head_view(): piece = lax.dynamic_slice_in_dim(matrix, index * columns, columns, 1)  18.6 us
    all_to_all x1, starting transfers between devices, shards(): lax.all_to_all(outgoing_at.reshape(curve_size, capacity), 'curve', split_...  18.4 us
    all_to_all x1, waiting for transfers between devices, shards(): lax.all_to_all(outgoing.reshape(curve_size, capacity, width), 'curve', sp...  16.6 us
    reduce_sum x4, other arithmetic, backward_group(): jnp.sum(weights * weight_grad, axis=-1, keepdims=True)  14.8 us
  transfers between devices with their start and end apart: 6, of which 5 were waited for; matrix products, arithmetic and copies ran while one was open for 16% of the time, Pallas kernels for 0%

commit v1 on v0

--- a/solution.py
+++ b/solution.py
@@ -79,7 +79,10 @@
     source_rows = points.reshape(count, width)
     packed, prep_pull = jax.vjp(lambda inputs: prepare(inputs, norm_gain_one, qkv_one), source_rows)
     queries = packed[:, :width]
-    gathered = lax.all_gather(packed[:, width:], "patch", axis=0, tiled=True)
+    gathered = jnp.concatenate(
+        lax.all_to_all(jnp.stack([packed[:, width:]] * lax.axis_size("patch")), "patch", 0, 0),
+        axis=0,
+    )
     keys_all = gathered[:, :width]
     values_all = gathered[:, width:]
     patch_len = gathered.shape[0]

time: 359 us -> 372 us (1.036)
  starting transfers between devices: 39.9 us -> 50.4 us
  local copies, waits for them, and re-layouts: 73.3 us -> 78.8 us
  waiting for transfers between devices: 119 us -> 115 us
    all_gather x1 -> x0, waiting for transfers between devices: 19.1 us -> none  [shards(): gathered = lax.all_gather(packed[:, width:], 'patch', axis=0, tiled=True)]
    all_to_all x0 -> x1, waiting for transfers between devices: none -> 15.8 us  [shards(): lax.all_to_all(jnp.stack([packed[:, width:]] * lax.axis_size('patch')), '...]
    all_to_all x1, starting transfers between devices: 18.4 us -> 24.6 us  [shards(): lax.all_to_all(outgoing_at.reshape(curve_size, capacity), 'curve', split_...]
    all_to_all x0 -> x1, starting transfers between devices: none -> 4.97 us  [shards(): lax.all_to_all(jnp.stack([packed[:, width:]] * lax.axis_size('patch')), '...]
    all_to_all x0 -> x1, local copies, waits for them, and re-layouts: none -> 3.98 us  [shards(): lax.all_to_all(jnp.stack([packed[:, width:]] * lax.axis_size('patch')), '...]
  transfers between devices with their start and end apart: 6 -> 6, of which waited for: 5 -> 5; matrix products, arithmetic and copies ran while one was open for 16% -> 17% of each run, Pallas kernels for 0% -> 0%
where the time goes in v1:
time: 372 us; the launch traced here: 369 us
  waiting for transfers between devices  115 us (31%)
  matrix products  80.1 us (22%)
  local copies, waits for them, and re-layouts  78.8 us (21%)
  starting transfers between devices  50.4 us (14%)
  other arithmetic  26.4 us (7%)
  between operations  13.8 us (4%)
  loops' own time  5.05 us (1%)
    reduce_scatter x1, waiting for transfers between devices, shards(): lax.psum_scatter(regroup(key_parts), 'patch', scatter_dimension=0, tiled=...  36.8 us
    reduce_scatter x1, waiting for transfers between devices, shards(): lax.psum_scatter(regroup(value_parts), 'patch', scatter_dimension=0, tile...  25.1 us
    all_to_all x1, starting transfers between devices, shards(): lax.all_to_all(outgoing_at.reshape(curve_size, capacity), 'curve', split_...  24.6 us
    all_to_all x1, waiting for transfers between devices, shards(): lax.all_to_all(returning.reshape(curve_size, capacity, width), 'curve', s...  19.7 us
    dynamic_slice x28, local copies, waits for them, and re-layouts, head_view(): piece = lax.dynamic_slice_in_dim(matrix, index * columns, columns, 1)  18.6 us
    all_to_all x1, waiting for transfers between devices, shards(): lax.all_to_all(outgoing.reshape(curve_size, capacity, width), 'curve', sp...  16.6 us
    all_to_all x1, waiting for transfers between devices, shards(): lax.all_to_all(jnp.stack([packed[:, width:]] * lax.axis_size('patch')), '...  15.8 us
    reduce_sum x4, other arithmetic, backward_group(): jnp.sum(weights * weight_grad, axis=-1, keepdims=True)  14.8 us
  transfers between devices with their start and end apart: 6, of which 5 were waited for; matrix products, arithmetic and copies ran while one was open for 17% of the time, Pallas kernels for 0%

profile of v1, /device:TPU:1, one launch (start us, length us, event | category | flops | bytes accessed | tf_op | source)
XLA Modules:
  0.0 369.4 jit_solution(11582776343853068389)
XLA Ops:
  7.8 2.1 convolution_convert_fusion.2
  13.5 5.0 %all-to-all-start.1 = ((bf16[4,256,1024]{1,2,0:T(8,128)(2,1)}), bf16[4,256,1024]{1,2,0:T(8,128)(2,1)}, u32[]{:S(2)}, u32[]{:S(2)}) async-start(bf16[4,256,1024]{1,2,0:T(8,128)(2,1)} %stack.2), calls=%async_computation.1 | async-start | bytes 4194304 | tf_op jit(solution)/shard_map/all_to_all | solution.py:83
  22.8 15.8 %all-to-all-done.1 = bf16[4,256,1024]{1,2,0:T(8,128)(2,1)} async-done(((bf16[4,256,1024]{1,2,0:T(8,128)(2,1)}), bf16[4,256,1024]{1,2,0:T(8,128)(2,1)}, u32[]{:S(2)}, u32[]{:S(2)}) %all-to-all-start.1) | async-done | bytes 2097184 | tf_op jit(solution)/shard_map/all_to_all | solution.py:83
  38.6 24.6 %all-to-all-start = ((s32[128,1,4]{2,1,0:T(1,128)}), s32[128,1,4]{2,1,0:T(1,128)S(1)}, u32[]{:S(2)}, u32[]{:S(2)}) async-start(s32[128,1,4]{2,1,0:T(1,128)} %bitcast.21), calls=%async_computation | async-start | bytes 131072 | tf_op jit(solution)/shard_map/all_to_all | solution.py:129
  63.2 4.0 %copy.75 = bf16[4,256,1024]{2,1,0:T(8,128)(2,1)} copy(bf16[4,256,1024]{1,2,0:T(8,128)(2,1)} %all-to-all-done.1) | data formatting | bytes 4194304 | tf_op jit(solution)/shard_map/all_to_all | solution.py:83
  67.1 3.0 fusion.100
  71.7 2.3 copy.78
  74.7 40.3 %while.24 = (s32[]{:T(128)}, bf16[4,256,128]{1,2,0:T(8,128)(2,1)}, s32[4]{0:T(128)S(1)}, bf16[1024,512]{0,1:T(8,128)(2,1)S(1)}, bf16[256,512]{0,1:T(8,128)(2,1)}...) while((s32[]{:T(128)}, bf16[4,256,128]{1,2,0:T(8,128)(2,1)}, ...), condition=%wide.region_6.7_spmd, body=%wide.region_3.6_spmd.sunk | while | flops 139461632 | bytes 10363059 | solution.py:101
  77.8 3.3 fusion.159
  81.1 3.0 fusion.160
  87.8 3.3 fusion.159
  91.2 3.0 fusion.160
  97.9 3.3 fusion.159
  101.3 3.0 fusion.160
  108.0 3.3 fusion.159
  111.3 3.0 fusion.160
  115.0 2.1 fusion.43
  117.1 2.1 scatter_custom_fusion.1
  120.2 14.2 %all-to-all-start.2 = ((bf16[128,4,512]{2,1,0:T(4,128)(2,1)}), bf16[128,4,512]{2,1,0:T(4,128)(2,1)}, u32[]{:S(2)}, u32[]{:S(2)}) async-start(bf16[128,4,512]{2,1,0:T(4,128)(2,1)} %reshape.366), calls=%async_computation.2 | async-start | bytes 1048576 | tf_op jit(solution)/shard_map/all_to_all | solution.py:122
  137.9 16.6 %all-to-all-done.2 = bf16[128,4,512]{2,1,0:T(4,128)(2,1)} async-done(((bf16[128,4,512]{2,1,0:T(4,128)(2,1)}), bf16[128,4,512]{2,1,0:T(4,128)(2,1)}, u32[]{:S(2)}, u32[]{:S(2)}) %all-to-all-start.2) | async-done | bytes 524320 | tf_op jit(solution)/shard_map/all_to_all | solution.py:122
  154.6 2.0 reshape.412
  156.6 2.9 scatter_custom_fusion.2
  161.2 1.8 copy.80
  164.7 1.8 copy.82
  166.6 3.0 convolution_convert_fusion.3
  169.6 4.5 %fusion.102 = (f32[16,256]{1,0:T(8,128)S(1)}, f32[16,256,256]{1,2,0:T(8,128)}) fusion(pred[256,256]{0,1:T(8,128)(4,1)} %broadcast_compare_fusion, bf16[256,16,32]{0,2,1:T(8,128)(2,1)} %bitcast.187, bf16[256,16,32]{0,2,1:T(8,128)(2,1)} %bitcast.189), kind=kOutput, calls=%fused_computation.171 | convolution fusion | flops 71303424 | bytes 4800512 | tf_op jit(solution)/shard_map/jvp()/sub | solution.py:32
  174.1 4.0 %divide_convert_fusion.2 = (bf16[16,256,256]{1,2,0:T(8,128)(2,1)S(1)}, f32[16,256]{1,0:T(8,128)S(1)}) fusion(f32[16,256,256]{1,2,0:T(8,128)} %get-tuple-element.217, f32[16,256]{1,0:T(8,128)S(1)} %get-tuple-element.216, f32[16,256]{1,0:T(8,128)S(1)} %multiply_divide_fusion, bf16[16,256,256]{1,2,0:T(8,128)(2,1)} %convolution_convert_fusion.3), kind=kLoop, calls=%fused_computation.58 | loop fusion | flops 6287360 | bytes 8437760 | tf_op jit(solution)/shard_map/jvp()/convert_element_type | solution.py:33
  182.7 2.6 gather_fusion
  187.9 6.6 %all-to-all-start.3 = ((bf16[128,4,512]{2,1,0:T(4,128)(2,1)}), bf16[128,4,512]{2,1,0:T(4,128)(2,1)}, u32[]{:S(2)}, u32[]{:S(2)}) async-start(bf16[128,4,512]{2,1,0:T(4,128)(2,1)} %select_select_fusion), calls=%async_computation.3 | async-start | bytes 1048576 | tf_op jit(solution)/shard_map/all_to_all | solution.py:153
  194.6 19.7 %all-to-all-done.3 = bf16[128,4,512]{2,1,0:T(4,128)(2,1)} async-done(((bf16[128,4,512]{2,1,0:T(4,128)(2,1)}), bf16[128,4,512]{2,1,0:T(4,128)(2,1)}, u32[]{:S(2)}, u32[]{:S(2)}) %all-to-all-start.3) | async-done | bytes 524320 | tf_op jit(solution)/shard_map/all_to_all | solution.py:153
  215.4 1.9 gather_fusion.1
  217.3 2.1 convolution_convert_fusion.5
  220.2 74.5 %while.25 = (s32[]{:T(128)}, bf16[4,256,128]{1,2,0:T(8,128)(2,1)}, f32[4,1024,128]{1,2,0:T(8,128)}, f32[4,1024,128]{1,2,0:T(8,128)}, s32[4]{0:T(128)S(1)}, /*ind...) while((s32[]{:T(128)}, bf16[4,256,128]{1,2,0:T(8,128)(2,1)}, ...), condition=%wide.region_18.19_spmd, body=%wide.region_14.18_spmd.sunk | while | flops 356515840 | bytes 60391696 | solution.py:190
  223.3 2.1 convolution_convert_fusion.12
  226.2 3.3 fusion.171
  229.6 3.7 %fusion.172 = f32[4,256]{1,0:T(4,128)S(1)} fusion(bf16[4,256,1024]{2,1,0:T(8,128)(2,1)} %convolution_convert_fusion.12, f32[4,256,1024]{2,1,0:T(8,128)} %get-tuple-element.326, f32[4,256]{1,0:T(4,128)S(1)} %get-tuple-element.327), kind=kLoop, calls=%fused_computation.21.clone.1 | loop fusion | flops 4193280 | bytes 6299648 | tf_op jit(solution)/shard_map/while/body/eval_jaxpr/reduce_sum | solution.py:177
  241.9 2.1 convolution_convert_fusion.12
  244.9 3.3 fusion.171
  248.2 3.7 %fusion.172 = f32[4,256]{1,0:T(4,128)S(1)} fusion(bf16[4,256,1024]{2,1,0:T(8,128)(2,1)} %convolution_convert_fusion.12, f32[4,256,1024]{2,1,0:T(8,128)} %get-tuple-element.326, f32[4,256]{1,0:T(4,128)S(1)} %get-tuple-element.327), kind=kLoop, calls=%fused_computation.21.clone.1 | loop fusion | flops 4193280 | bytes 6299648 | tf_op jit(solution)/shard_map/while/body/eval_jaxpr/reduce_sum | solution.py:177
  260.5 2.1 convolution_convert_fusion.12
  263.5 3.3 fusion.171
  266.8 3.7 %fusion.172 = f32[4,256]{1,0:T(4,128)S(1)} fusion(bf16[4,256,1024]{2,1,0:T(8,128)(2,1)} %convolution_convert_fusion.12, f32[4,256,1024]{2,1,0:T(8,128)} %get-tuple-element.326, f32[4,256]{1,0:T(4,128)S(1)} %get-tuple-element.327), kind=kLoop, calls=%fused_computation.21.clone.1 | loop fusion | flops 4193280 | bytes 6299648 | tf_op jit(solution)/shard_map/while/body/eval_jaxpr/reduce_sum | solution.py:177
  279.1 2.1 convolution_convert_fusion.12
  282.1 3.4 fusion.171
  285.4 3.7 %fusion.172 = f32[4,256]{1,0:T(4,128)S(1)} fusion(bf16[4,256,1024]{2,1,0:T(8,128)(2,1)} %convolution_convert_fusion.12, f32[4,256,1024]{2,1,0:T(8,128)} %get-tuple-element.326, f32[4,256]{1,0:T(4,128)S(1)} %get-tuple-element.327), kind=kLoop, calls=%fused_computation.21.clone.1 | loop fusion | flops 4193280 | bytes 6299648 | tf_op jit(solution)/shard_map/while/body/eval_jaxpr/reduce_sum | solution.py:177
  295.4 25.1 %reduce-scatter.5.cloned.1.call-done = f32[256,512]{0,1:T(8,128)} async-done(((f32[1024,512]{0,1:T(8,128)}), f32[256,512]{0,1:T(8,128)}) %reduce-scatter.5.cloned.1.call-update) | async-done | bytes 524304 | tf_op jit(solution)/shard_map/reduce_scatter | solution.py:194
  321.6 36.8 %reduce-scatter.3.cloned.1.call-done = f32[256,512]{0,1:T(8,128)} async-done(((f32[1024,512]{0,1:T(8,128)}), f32[256,512]{0,1:T(8,128)}) %reduce-scatter.3.cloned.1.call-update) | async-done | bytes 524304 | tf_op jit(solution)/shard_map/reduce_scatter | solution.py:193
  359.5 2.1 fusion.68
  (175 shorter events, 79.7 us)
Async XLA Ops:
  6.5 153.1 %copy-start = (bf16[512,1536]{1,0:T(8,128)(2,1)S(1)}, bf16[512,1536]{1,0:T(8,128)(2,1)}, u32[]{:S(2)}) copy-start(bf16[512,1536]{1,0:T(8,128)(2,1)} %param.20) | copy-start | bytes 4718596
  7.7 3.0 copy-start.16
  7.8 3.0 copy-start.14
  10.8 7.7 %copy-start.18 = (s32[1,1,256]{2,1,0:T(1,128)S(1)}, s32[1,1,256]{2,1,0:T(1,128)}, u32[]{:S(2)}) copy-start(s32[1,1,256]{2,1,0:T(1,128)} %param.18) | copy-start | bytes 3076
  12.0 9.7 %copy-start.7 = (bf16[1,1,256,512]{3,2,1,0:T(8,128)(2,1)S(1)}, bf16[1,1,256,512]{3,2,1,0:T(8,128)(2,1)}, u32[]{:S(2)}) copy-start(bf16[1,1,256,512]{3,2,1,0:T(8,128)(2,1)} %param.23) | copy-start | bytes 786436
  13.5 8.3 %copy-start.9 = (bf16[512,512]{1,0:T(8,128)(2,1)S(1)}, bf16[512,512]{1,0:T(8,128)(2,1)}, u32[]{:S(2)}) copy-start(bf16[512,512]{1,0:T(8,128)(2,1)} %param.21) | copy-start | bytes 1572868
  13.5 25.1 %all-to-all-start.1 = ((bf16[4,256,1024]{1,2,0:T(8,128)(2,1)}), bf16[4,256,1024]{1,2,0:T(8,128)(2,1)}, u32[]{:S(2)}, u32[]{:S(2)}) async-start(bf16[4,256,1024]{1,2,0:T(8,128)(2,1)} %stack.2), calls=%async_computation.1 | async-start | bytes 4194304 | tf_op jit(solution)/shard_map/all_to_all | solution.py:83
  38.6 81.6 %all-to-all-start = ((s32[128,1,4]{2,1,0:T(1,128)}), s32[128,1,4]{2,1,0:T(1,128)S(1)}, u32[]{:S(2)}, u32[]{:S(2)}) async-start(s32[128,1,4]{2,1,0:T(1,128)} %bitcast.21), calls=%async_computation | async-start | bytes 131072 | tf_op jit(solution)/shard_map/all_to_all | solution.py:129
  74.7 40.3 %copy-start.5 = (bf16[1,1,256,512]{3,2,1,0:T(8,128)(2,1)S(1)}, bf16[1,1,256,512]{3,2,1,0:T(8,128)(2,1)}, u32[]{:S(2)}) copy-start(bf16[1,1,256,512]{3,2,1,0:T(8,128)(2,1)} %param.14) | copy-start | bytes 786436
  74.7 59.7 %copy-start.19 = (s32[1,1,256]{2,1,0:T(1,128)S(1)}, s32[1,1,256]{2,1,0:T(1,128)}, u32[]{:S(2)}) copy-start(s32[1,1,256]{2,1,0:T(1,128)} %param.22) | copy-start | bytes 3076
  115.0 44.6 %copy-start.20 = (f32[512]{0:T(512)S(1)}, f32[512]{0:T(512)}, u32[]{:S(2)}) copy-start(f32[512]{0:T(512)} %param.19) | copy-start | bytes 6148
  120.2 34.4 %all-to-all-start.2 = ((bf16[128,4,512]{2,1,0:T(4,128)(2,1)}), bf16[128,4,512]{2,1,0:T(4,128)(2,1)}, u32[]{:S(2)}, u32[]{:S(2)}) async-start(bf16[128,4,512]{2,1,0:T(4,128)(2,1)} %reshape.366), calls=%async_computation.2 | async-start | bytes 1048576 | tf_op jit(solution)/shard_map/all_to_all | solution.py:122
  174.0 4.0 %copy-start.3 = (bf16[16,256,256]{1,2,0:T(8,128)(2,1)S(1)}, bf16[16,256,256]{1,2,0:T(8,128)(2,1)}, u32[]{:S(2)}) copy-start(bf16[16,256,256]{1,2,0:T(8,128)(2,1)} %convolution_convert_fusion.3) | copy-start | bytes 6291460
  174.1 4.7 %copy-start.4 = (f32[16,256,256]{1,2,0:T(8,128)S(1)}, f32[16,256,256]{1,2,0:T(8,128)}, u32[]{:S(2)}) copy-start(f32[16,256,256]{1,2,0:T(8,128)} %get-tuple-element.217) | copy-start | bytes 12582916
  174.1 4.7 %copy-start.11 = (bf16[256,512]{0,1:T(8,128)(2,1)S(1)}, bf16[256,512]{0,1:T(8,128)(2,1)}, u32[]{:S(2)}) copy-start(bf16[256,512]{0,1:T(8,128)(2,1)} %copy.80) | copy-start | bytes 786436
  174.1 4.7 %copy-start.13 = (pred[256,256]{0,1:T(8,128)(4,1)S(1)}, pred[256,256]{0,1:T(8,128)(4,1)}, u32[]{:S(2)}) copy-start(pred[256,256]{0,1:T(8,128)(4,1)} %broadcast_compare_fusion) | copy-start | bytes 196612
  178.7 1.2 copy-start.10
  181.1 1.5 copy-start.8
  187.9 26.4 %all-to-all-start.3 = ((bf16[128,4,512]{2,1,0:T(4,128)(2,1)}), bf16[128,4,512]{2,1,0:T(4,128)(2,1)}, u32[]{:S(2)}, u32[]{:S(2)}) async-start(bf16[128,4,512]{2,1,0:T(4,128)(2,1)} %select_select_fusion), calls=%async_computation.3 | async-start | bytes 1048576 | tf_op jit(solution)/shard_map/all_to_all | solution.py:153
  194.5 126.0 %reduce-scatter.5.cloned.1.call-start = ((), (), s32[]{:S(2)}) async-start(), calls=%async_computation.7 | async-start | bytes 2621440 | tf_op jit(solution)/shard_map/reduce_scatter | solution.py:194
  229.6 3.7 %copy-start.1 = (bf16[4,256,1024]{2,1,0:T(8,128)(2,1)S(1)}, bf16[4,256,1024]{2,1,0:T(8,128)(2,1)}, u32[]{:S(2)}) copy-start(bf16[4,256,1024]{2,1,0:T(8,128)(2,1)} %convolution_convert_fusion.12) | copy-start | bytes 6291460 | tf_op jit(solution)/shard_map/while
  229.6 4.7 %copy-start.2 = (f32[4,256,1024]{2,1,0:T(8,128)S(1)}, f32[4,256,1024]{2,1,0:T(8,128)}, u32[]{:S(2)}) copy-start(f32[4,256,1024]{2,1,0:T(8,128)} %get-tuple-element.326) | copy-start | bytes 12582916 | tf_op jit(solution)/shard_map/while
  248.2 3.7 %copy-start.1 = (bf16[4,256,1024]{2,1,0:T(8,128)(2,1)S(1)}, bf16[4,256,1024]{2,1,0:T(8,128)(2,1)}, u32[]{:S(2)}) copy-start(bf16[4,256,1024]{2,1,0:T(8,128)(2,1)} %convolution_convert_fusion.12) | copy-start | bytes 6291460 | tf_op jit(solution)/shard_map/while
  248.2 4.7 %copy-start.2 = (f32[4,256,1024]{2,1,0:T(8,128)S(1)}, f32[4,256,1024]{2,1,0:T(8,128)}, u32[]{:S(2)}) copy-start(f32[4,256,1024]{2,1,0:T(8,128)} %get-tuple-element.326) | copy-start | bytes 12582916 | tf_op jit(solution)/shard_map/while
  266.8 3.7 %copy-start.1 = (bf16[4,256,1024]{2,1,0:T(8,128)(2,1)S(1)}, bf16[4,256,1024]{2,1,0:T(8,128)(2,1)}, u32[]{:S(2)}) copy-start(bf16[4,256,1024]{2,1,0:T(8,128)(2,1)} %convolution_convert_fusion.12) | copy-start | bytes 6291460 | tf_op jit(solution)/shard_map/while
  266.8 4.7 %copy-start.2 = (f32[4,256,1024]{2,1,0:T(8,128)S(1)}, f32[4,256,1024]{2,1,0:T(8,128)}, u32[]{:S(2)}) copy-start(f32[4,256,1024]{2,1,0:T(8,128)} %get-tuple-element.326) | copy-start | bytes 12582916 | tf_op jit(solution)/shard_map/while
  285.4 3.7 %copy-start.1 = (bf16[4,256,1024]{2,1,0:T(8,128)(2,1)S(1)}, bf16[4,256,1024]{2,1,0:T(8,128)(2,1)}, u32[]{:S(2)}) copy-start(bf16[4,256,1024]{2,1,0:T(8,128)(2,1)} %convolution_convert_fusion.12) | copy-start | bytes 6291460 | tf_op jit(solution)/shard_map/while
  285.4 4.7 %copy-start.2 = (f32[4,256,1024]{2,1,0:T(8,128)S(1)}, f32[4,256,1024]{2,1,0:T(8,128)}, u32[]{:S(2)}) copy-start(f32[4,256,1024]{2,1,0:T(8,128)} %get-tuple-element.326) | copy-start | bytes 12582916 | tf_op jit(solution)/shard_map/while
  294.6 64.9 %copy-start.12 = (bf16[4,256,128]{1,2,0:T(8,128)(2,1)S(1)}, bf16[4,256,128]{1,2,0:T(8,128)(2,1)}, u32[]{:S(2)}) copy-start(bf16[4,256,128]{1,2,0:T(8,128)(2,1)} %get-tuple-element.87) | copy-start | bytes 786436
  294.6 64.9 %copy-start.21 = (f32[512]{0:T(512)S(1)}, f32[512]{0:T(512)}, u32[]{:S(2)}) copy-start(f32[512]{0:T(512)} %param.15) | copy-start | bytes 6148
  294.7 66.9 %copy-start.17 = (f32[256]{0:T(256)S(1)}, f32[256]{0:T(256)}, u32[]{:S(2)}) copy-start(f32[256]{0:T(256)} %copy-done.16) | copy-start | bytes 3076
  294.7 67.0 %copy-start.6 = (bf16[256,512]{1,0:T(8,128)(2,1)S(1)}, bf16[256,512]{1,0:T(8,128)(2,1)}, u32[]{:S(2)}) copy-start(bf16[256,512]{1,0:T(8,128)(2,1)} %gather_fusion.1) | copy-start | bytes 786436
  294.7 67.0 %copy-start.15 = (f32[256]{0:T(256)S(1)}, f32[256]{0:T(256)}, u32[]{:S(2)}) copy-start(f32[256]{0:T(256)} %copy-done.14) | copy-start | bytes 3076
  294.7 63.7 %reduce-scatter.3.cloned.1.call-start = ((), (), s32[]{:S(2)}) async-start(), calls=%async_computation.6 | async-start | bytes 2621440 | tf_op jit(solution)/shard_map/reduce_scatter | solution.py:193
Sparse Core Ops, SparseCore 0:
  294.8 25.6 reduce-scatter.4
  323.6 34.7 reduce-scatter.2
